TPU v7x, 32 devices: a whole 2x2x4 slice. The times are simulated.
32 devices in a mesh: row: 8 (over z, y), col: 4 (over x, core).
Axes of the slice: x: 2, y: 2, z: 4, core: 2. Of those that a mesh axis runs over, the one named last changes fastest.
Arguments:
- a_blocks: float32 [128, 8, 125, 125], P('row', 'col'), may hold values from -0.1875 to 0.1875
- a_pattern: int32 [128, 8], P('row', 'col'), may hold values 0 or 1
- row_owner: int32 [128], replicated, may hold values from 0 to 127, as said below
- prolong: float32 [8, 24, 125, 125], P('row', 'col'), may hold values from -6 to 6
- p_pattern: int32 [8, 24], P('row', 'col'), may hold values 0 or 1
- prolong_slab: float32 [128, 8, 125, 125], P('row'), may hold values from -0.0625 to 0.0625
Outputs:
- coarse: float32 [8, 24, 125, 125], P('row', 'col')
Inputs may be any that keep to these rules, and one draw needn't show every extreme that they name: row_owner is a permutation; the 16 element-order rows e with e // 16 equal go to at most 2 positions p of any one value p // 16, and exactly 2 for each value they reach.
All inputs are finite; a program needn't handle non-finite values. No bound on the sum of `a_pattern` or of `p_pattern` on one device may be relied on, other than what follows from the above.
Results may differ from a plain program's by a relative error of at most 0.0001.
Values sent between devices are 32-bit elements; how exact they have to be, the bound alone decides.
A program may use at most 128 MiB of HBM per device.

v0:
```python
import jax
import jax.numpy as jnp
from jax import lax
from jax.sharding import PartitionSpec as P

CAP = 2


def ranks_of(targets):
    width = targets.shape[-1]
    same = targets[..., :, None] == targets[..., None, :]
    lower = jnp.arange(width)[:, None] > jnp.arange(width)[None, :]
    return jnp.sum(jnp.where(same & lower, 1, 0), axis=-1).astype(jnp.int32)


def pick(rows, at):
    return jnp.stack(
        [lax.dynamic_index_in_dim(rows, at[i], 0, keepdims=False) for i in range(at.shape[0])]
    )


def shards(a_blocks, a_pattern, row_owner, prolong, p_pattern, prolong_slab):
    width = a_blocks.shape[0]
    count = lax.axis_size("row")
    me = lax.axis_index("row")
    masked = a_blocks * a_pattern.astype(jnp.float32)[:, :, None, None]
    p_masked = prolong * p_pattern.astype(jnp.float32)[:, :, None, None]
    p_full = lax.all_gather(p_masked, "row", axis=0, tiled=True)
    table = row_owner.reshape(count, width)
    ranks = ranks_of(table // width)
    targets = lax.dynamic_index_in_dim(table, me, 0, keepdims=False) // width
    mine = lax.dynamic_index_in_dim(ranks, me, 0, keepdims=False)
    slot = targets * CAP + mine
    hit = slot[None, :] == jnp.arange(count * CAP, dtype=jnp.int32)[:, None]
    order = jnp.sum(jnp.where(hit, jnp.arange(width, dtype=jnp.int32)[None, :], 0), axis=1)
    packed = pick(masked, order)
    packed = packed.reshape((count, CAP) + masked.shape[1:])
    received = lax.all_to_all(packed, "row", split_axis=0, concat_axis=0, tiled=True)
    received = received.reshape((count * CAP,) + masked.shape[1:])
    wanted = table[None] == (me * width + jnp.arange(width, dtype=jnp.int32))[:, None, None]
    source = jnp.arange(count, dtype=jnp.int32)[:, None] * CAP + ranks
    where = jnp.sum(jnp.where(wanted, source[None], 0), axis=(1, 2))
    grid_a = pick(received, where)
    part = jnp.einsum(
        "maxy,mkxz->akyz",
        prolong_slab,
        grid_a,
        precision=lax.Precision.HIGH,
        preferred_element_type=jnp.float32,
    )
    mine = lax.psum_scatter(part, "row", scatter_dimension=0, tiled=True)
    mid = lax.all_gather(mine, "col", axis=1, tiled=True)
    return jnp.einsum(
        "akyx,knxz->anyz",
        mid,
        p_full,
        precision=lax.Precision.HIGH,
        preferred_element_type=jnp.float32,
    )


def solution(mesh):
    in_specs = (
        P("row", "col", None, None),
        P("row", "col"),
        P(),
        P("row", "col", None, None),
        P("row", "col"),
        P("row", None, None, None),
    )
    out_specs = P("row", "col", None, None)
    return jax.shard_map(shards, mesh=mesh, in_specs=in_specs, out_specs=out_specs, check_vma=False)
```

profile of v0, /device:TPU:0, one launch (start us, length us, event | category | flops | bytes accessed | tf_op | source)
XLA Modules:
  0.0 269.7 jit_solution(4542487792375120371)
XLA Ops:
  6.5 0.7 reshape.110
  7.7 0.7 fusion.16
  28.4 0.7 convert_element_type.7
  29.8 2.3 broadcast_multiply_fusion
  32.1 0.7 dynamic-slice_dynamic-update-slice_fusion.31
  33.4 0.7 dynamic-slice_dynamic-update-slice_fusion.30
  34.6 0.7 dynamic-slice_dynamic-update-slice_fusion.29
  35.9 0.7 dynamic-slice_dynamic-update-slice_fusion.28
  38.5 0.7 dynamic-slice_dynamic-update-slice_fusion.26
  39.8 0.7 dynamic-slice_dynamic-update-slice_fusion.25
  41.2 0.7 dynamic-slice_dynamic-update-slice_fusion.24
  42.4 0.7 dynamic-slice_dynamic-update-slice_fusion.23
  43.8 0.7 dynamic-slice_dynamic-update-slice_fusion.22
  45.0 0.7 dynamic-slice_dynamic-update-slice_fusion.21
  46.3 0.7 dynamic-slice_dynamic-update-slice_fusion.20
  47.6 0.7 dynamic-slice_dynamic-update-slice_fusion.19
  48.9 0.7 dynamic-slice_dynamic-update-slice_fusion.18
  50.2 0.7 dynamic-slice_dynamic-update-slice_fusion.17
  51.5 0.7 dynamic-slice_dynamic-update-slice_fusion.16
  52.2 7.3 %all-to-all-start = ((f32[8,2,2,125,125]{4,2,3,1,0:T(2,128)}), f32[8,2,2,125,125]{4,2,3,1,0:T(2,128)}, u32[]{:S(2)}, u32[]{:S(2)}) async-start(f32[8,2,2,125,125]{4,2,3,1,0:T(2,128)} %bitcast.84), calls=%async_computation | async-start | bytes 4096000 | tf_op jit(solution)/shard_map/all_to_all | solution.py:38
  60.0 0.7 fusion.15
  90.4 16.4 %all-to-all-done = f32[8,2,2,125,125]{4,2,3,1,0:T(2,128)} async-done(((f32[8,2,2,125,125]{4,2,3,1,0:T(2,128)}), f32[8,2,2,125,125]{4,2,3,1,0:T(2,128)}, u32[]{:S(2)}, u32[]{:S(2)}) %all-to-all-start) | async-done | bytes 2000032 | tf_op jit(solution)/shard_map/all_to_all | solution.py:38
  106.7 2.8 %copy.31 = f32[8,2,2,125,125]{3,4,1,0,2:T(8,128)S(1)} copy(f32[8,2,2,125,125]{4,2,3,1,0:T(2,128)} %all-to-all-done) | data formatting | bytes 4000000 | tf_op jit(solution)/shard_map/all_to_all | solution.py:38
  110.0 8.5 %fusion.4 = f32[8,2,125,125]{2,3,0,1:T(8,128)S(1)} fusion(f32[16,8,125,125]{3,1,2,0:T(8,128)} %param.11, f32[16,2,125,125]{2,3,0,1:T(8,128)S(1)} %dynamic-slice_dynamic-update-slice_fusion), kind=kOutput, calls=%fused_computation.4 | convolution fusion | flops 3000000000 | bytes 11000000 | tf_op jit(solution)/shard_map/maxy,mkxz->akyz/dot_general | solution.py:44
  118.5 1.4 copy.33
  120.4 0.8 broadcast_multiply_fusion.1
  121.9 75.0 %all-reduce.3.cloned.1.call-done = f32[8,2,125,125]{3,1,2,0:T(2,128)} async-done(((f32[8,2,125,125]{3,1,2,0:T(2,128)}), f32[8,2,125,125]{3,1,2,0:T(2,128)}) %all-reduce.3.cloned.1.call-update) | async-done | bytes 1000016
  196.9 1.6 constant_dynamic-slice_fusion.2
  198.6 7.1 %all_gather.7 = f32[1,8,125,125]{3,0,2,1:T(1,128)S(1)} all-gather(f32[1,2,125,125]{3,0,2,1:T(1,128)S(1)} %copy.34), channel_id=1, replica_groups=mesh['row'=8,'col'=4] {'col'}, dimensions={1}, use_global_device_ids=true | all-gather | bytes 625000 | tf_op jit(solution)/shard_map/all_gather | solution.py:52
  205.7 52.9 %all-gather.2.cloned.1.call-done = f32[8,6,125,125]{2,3,0,1:T(8,128)} async-done(((f32[1,6,125,125]{2,3,0,1:T(8,128)}), f32[8,6,125,125]{2,3,0,1:T(8,128)}) %all-gather.2.cloned.1.call-update) | async-done | bytes 3000016 | tf_op jit(solution)/shard_map/all_gather | solution.py:28
  258.6 3.3 %convolution_bitcast_fusion = f32[1,6,125,125]{2,3,1,0:T(8,128)S(1)} fusion(f32[8,6,125,125]{2,3,0,1:T(8,128)} %all-gather.2.cloned.1.call-done, f32[1,8,125,125]{3,0,2,1:T(1,128)S(1)} %all_gather.7), kind=kOutput, calls=%fused_computation.5 | convolution fusion | flops 562499968 | bytes 3875000 | tf_op jit(solution)/shard_map/akyx,knxz->anyz/dot_general | solution.py:53
  261.9 1.0 copy.37
  (41 shorter events, 3.2 us)
Async XLA Ops:
  52.2 54.6 %all-to-all-start = ((f32[8,2,2,125,125]{4,2,3,1,0:T(2,128)}), f32[8,2,2,125,125]{4,2,3,1,0:T(2,128)}, u32[]{:S(2)}, u32[]{:S(2)}) async-start(f32[8,2,2,125,125]{4,2,3,1,0:T(2,128)} %bitcast.84), calls=%async_computation | async-start | bytes 4096000 | tf_op jit(solution)/shard_map/all_to_all | solution.py:38
  59.4 137.5 %all-reduce.3.cloned.1.call-start = ((), (), s32[]{:S(2)}) async-start(), calls=%async_computation.2 | async-start | bytes 2048000
  118.5 1.5 copy-start
  118.5 1.9 copy-start.1
  118.5 2.7 %copy-start.2 = (u32[32]{0:T(128)S(1)}, u32[32]{0:T(128)}, u32[]{:S(2)}) copy-start(u32[32]{0:T(128)} %constant.116) | copy-start | bytes 388
  119.9 138.6 %all-gather.2.cloned.1.call-start = ((), (), s32[]{:S(2)}) async-start(), calls=%async_computation.1 | async-start | bytes 3538944 | tf_op jit(solution)/shard_map/all_gather | solution.py:28
Sparse Core Ops, SparseCore 0:
  120.1 76.7 all-reduce.2
  199.1 59.4 all-gather.1
where the time goes:
time: 271 us; the launch traced here: 270 us
  waiting for transfers between devices  144 us (53%)
  between operations  73.3 us (27%)
  local copies, waits for them, and re-layouts  21.1 us (8%)
  matrix products  11.8 us (4%)
  starting transfers between devices  7.36 us (3%)
  blocking collectives  7.08 us (3%)
  other arithmetic  4.83 us (2%)
    unnamed x3, waiting for transfers between devices  75.1 us
    all_gather x1, waiting for transfers between devices, shards(): p_full = lax.all_gather(p_masked, 'row', axis=0, tiled=True)  52.9 us
    all_to_all x1, waiting for transfers between devices, shards(): lax.all_to_all(packed, 'row', split_axis=0, concat_axis=0, tiled=True)  16.4 us
    unnamed x39, local copies, waits for them, and re-layouts  12.8 us
    dot_general x1, matrix products, shards(): jnp.einsum('maxy,mkxz->akyz', prolong_slab, grid_a, precision=lax.Precisi...  8.49 us
    all_to_all x1, starting transfers between devices, shards(): lax.all_to_all(packed, 'row', split_axis=0, concat_axis=0, tiled=True)  7.28 us
    all_gather x1, blocking collectives, shards(): mid = lax.all_gather(mine, 'col', axis=1, tiled=True)  7.08 us
  transfers between devices with their start and end apart: 3, of which 3 were waited for; matrix products, arithmetic and copies ran while one was open for 2% of the time, Pallas kernels for 0%

commit v1 on v0

--- a/solution.py
+++ b/solution.py
@@ -4,6 +4,22 @@
 from jax.sharding import PartitionSpec as P
 
 CAP = 2
+
+
+def ring_product(x, axis, dim, term):
+    count, position, rows = (lax.axis_size(axis), lax.axis_index(axis), x.shape[dim])
+    right = [(i, (i + 1) % count) for i in range(count)]
+    behind = [(i, (i - 1) % count) for i in range(count)]
+    middle = count // 2
+    from_left = from_right = x
+    so_far = term(x, position * rows)
+    for hop in range(1, middle + 1):
+        from_left = lax.ppermute(from_left, axis, right)
+        if hop < count - middle:
+            from_right = lax.ppermute(from_right, axis, behind)
+            so_far = so_far + term(from_right, (position + hop) % count * rows)
+        so_far = so_far + term(from_left, (position - hop) % count * rows)
+    return so_far
 
 
 def ranks_of(targets):
@@ -25,7 +41,6 @@
     me = lax.axis_index("row")
     masked = a_blocks * a_pattern.astype(jnp.float32)[:, :, None, None]
     p_masked = prolong * p_pattern.astype(jnp.float32)[:, :, None, None]
-    p_full = lax.all_gather(p_masked, "row", axis=0, tiled=True)
     table = row_owner.reshape(count, width)
     ranks = ranks_of(table // width)
     targets = lax.dynamic_index_in_dim(table, me, 0, keepdims=False) // width
@@ -50,12 +65,17 @@
     )
     mine = lax.psum_scatter(part, "row", scatter_dimension=0, tiled=True)
     mid = lax.all_gather(mine, "col", axis=1, tiled=True)
-    return jnp.einsum(
-        "akyx,knxz->anyz",
-        mid,
-        p_full,
-        precision=lax.Precision.HIGH,
-        preferred_element_type=jnp.float32,
+    return ring_product(
+        p_masked,
+        "row",
+        0,
+        lambda part_2, offset: jnp.einsum(
+            "akyx,knxz->anyz",
+            lax.dynamic_slice_in_dim(mid, offset, part_2.shape[0], axis=1),
+            part_2,
+            precision=lax.Precision.HIGH,
+            preferred_element_type=jnp.float32,
+        ),
     )
 
 

time: 271 us -> 248 us (0.915)
  waiting for transfers between devices: 144 us -> 105 us
  starting transfers between devices: 7.36 us -> 24.8 us
    all_gather x1 -> x0, waiting for transfers between devices: 52.9 us -> none  [shards(): p_full = lax.all_gather(p_masked, 'row', axis=0, tiled=True)]
    ppermute x0 -> x7, waiting for transfers between devices: none -> 46.4 us  [the longest x4 26.6 us: ring_product(): from_left = lax.ppermute(from_left, axis, right)]
    unnamed x3 -> x2, waiting for transfers between devices: 75.1 us -> 44.5 us
    ppermute x0 -> x7, starting transfers between devices: none -> 17.4 us  [the longest x4 14.6 us: ring_product(): from_left = lax.ppermute(from_left, axis, right)]
  transfers between devices with their start and end apart: 3 -> 9, of which waited for: 3 -> 6; matrix products, arithmetic and copies ran while one was open for 2% -> 8% of each run, Pallas kernels for 0% -> 0%
where the time goes in v1:
time: 248 us; the launch traced here: 247 us
  waiting for transfers between devices  105 us (42%)
  between operations  73.6 us (30%)
  starting transfers between devices  24.8 us (10%)
  local copies, waits for them, and re-layouts  21.1 us (9%)
  matrix products  11.1 us (4%)
  blocking collectives  7.08 us (3%)
  other arithmetic  4.08 us (2%)
    unnamed x2, waiting for transfers between devices  44.5 us
    ppermute x4, waiting for transfers between devices, ring_product(): from_left = lax.ppermute(from_left, axis, right)  26.6 us
    ppermute x3, waiting for transfers between devices, ring_product(): from_right = lax.ppermute(from_right, axis, behind)  19.8 us
    ppermute x4, starting transfers between devices, ring_product(): from_left = lax.ppermute(from_left, axis, right)  14.6 us
    all_to_all x1, waiting for transfers between devices, shards(): lax.all_to_all(packed, 'row', split_axis=0, concat_axis=0, tiled=True)  13.7 us
    unnamed x39, local copies, waits for them, and re-layouts  12.7 us
    dot_general x1, matrix products, shards(): jnp.einsum('maxy,mkxz->akyz', prolong_slab, grid_a, precision=lax.Precisi...  8.49 us
    all_to_all x1, starting transfers between devices, shards(): lax.all_to_all(packed, 'row', split_axis=0, concat_axis=0, tiled=True)  7.41 us
  transfers between devices with their start and end apart: 9, of which 6 were waited for; matrix products, arithmetic and copies ran while one was open for 8% of the time, Pallas kernels for 0%

profile of v1, /device:TPU:0, one launch (start us, length us, event | category | flops | bytes accessed | tf_op | source)
XLA Modules:
  0.0 246.5 jit_solution(9653345517566798977)
XLA Ops:
  6.5 0.7 reshape.166
  7.7 0.7 fusion.28
  28.5 0.7 convert_element_type.7
  29.8 2.3 broadcast_multiply_fusion
  32.2 0.7 dynamic-slice_dynamic-update-slice_fusion.31
  34.9 0.7 dynamic-slice_dynamic-update-slice_fusion.29
  37.4 0.7 dynamic-slice_dynamic-update-slice_fusion.27
  38.7 0.7 dynamic-slice_dynamic-update-slice_fusion.26
  40.0 0.7 dynamic-slice_dynamic-update-slice_fusion.25
  41.2 0.7 dynamic-slice_dynamic-update-slice_fusion.24
  43.8 0.7 dynamic-slice_dynamic-update-slice_fusion.22
  45.1 0.7 dynamic-slice_dynamic-update-slice_fusion.21
  51.7 0.7 dynamic-slice_dynamic-update-slice_fusion.16
  52.3 7.4 %all-to-all-start = ((f32[8,2,2,125,125]{4,2,3,1,0:T(2,128)}), f32[8,2,2,125,125]{4,2,3,1,0:T(2,128)}, u32[]{:S(2)}, u32[]{:S(2)}) async-start(f32[8,2,2,125,125]{4,2,3,1,0:T(2,128)} %bitcast.140), calls=%async_computation | async-start | bytes 4096000 | tf_op jit(solution)/shard_map/all_to_all | solution.py:53
  60.3 2.0 collective-permute-start.1
  62.9 0.7 fusion.27
  93.3 13.7 %all-to-all-done = f32[8,2,2,125,125]{4,2,3,1,0:T(2,128)} async-done(((f32[8,2,2,125,125]{4,2,3,1,0:T(2,128)}), f32[8,2,2,125,125]{4,2,3,1,0:T(2,128)}, u32[]{:S(2)}, u32[]{:S(2)}) %all-to-all-start) | async-done | bytes 2000032 | tf_op jit(solution)/shard_map/all_to_all | solution.py:53
  107.1 2.8 %copy.42 = f32[8,2,2,125,125]{3,4,1,0,2:T(8,128)S(1)} copy(f32[8,2,2,125,125]{4,2,3,1,0:T(2,128)} %all-to-all-done) | data formatting | bytes 4000000 | tf_op jit(solution)/shard_map/all_to_all | solution.py:53
  110.3 8.5 %fusion.4 = f32[8,2,125,125]{2,3,0,1:T(8,128)S(1)} fusion(f32[16,8,125,125]{3,1,2,0:T(8,128)} %param.11, f32[16,2,125,125]{2,3,0,1:T(8,128)S(1)} %dynamic-slice_dynamic-update-slice_fusion), kind=kOutput, calls=%fused_computation.4 | convolution fusion | flops 3000000000 | bytes 11000000 | tf_op jit(solution)/shard_map/maxy,mkxz->akyz/dot_general | solution.py:59
  118.8 1.3 copy.44
  120.2 2.5 %collective-permute-start = (f32[1,6,125,125]{2,3,1,0:T(8,128)S(1)}, f32[1,6,125,125]{2,3,1,0:T(8,128)S(1)}, u32[]{:S(2)}, u32[]{:S(2)}) collective-permute-start(f32[1,6,125,125]{2,3,1,0:T(8,128)S(1)} %broadcast_multiply_fusion.1), channel_id=1, source_target_pairs={{0,28},{4,0},{8,4},{12,8},{16,12},{20,16},{24,20},{28,24},{1,29},{... | collective-permute-start | bytes 1125008 | tf_op jit(solution)/shard_map/ppermute | solution.py:19
  122.7 7.5 %collective-permute-start.3 = (f32[1,6,125,125]{2,3,1,0:T(8,128)S(1)}, f32[1,6,125,125]{2,3,1,0:T(8,128)S(1)}, u32[]{:S(2)}, u32[]{:S(2)}) collective-permute-start(f32[1,6,125,125]{2,3,1,0:T(8,128)S(1)} %collective-permute-done.1), channel_id=1, source_target_pairs={{0,4},{4,8},{8,12},{12,16},{16,20},{20,24},{24,28},{28,0},{1,5},{5... | collective-permute-start | bytes 1125008 | tf_op jit(solution)/shard_map/ppermute | solution.py:17
  130.2 18.0 %collective-permute-done = f32[1,6,125,125]{2,3,1,0:T(8,128)S(1)} collective-permute-done((f32[1,6,125,125]{2,3,1,0:T(8,128)S(1)}, f32[1,6,125,125]{2,3,1,0:T(8,128)S(1)}, u32[]{:S(2)}, u32[]{:S(2)}) %collective-permute-start) | collective-permute-done | bytes 375032 | tf_op jit(solution)/shard_map/ppermute | solution.py:19
  148.2 10.3 %collective-permute-done.3 = f32[1,6,125,125]{2,3,1,0:T(8,128)S(1)} collective-permute-done((f32[1,6,125,125]{2,3,1,0:T(8,128)S(1)}, f32[1,6,125,125]{2,3,1,0:T(8,128)S(1)}, u32[]{:S(2)}, u32[]{:S(2)}) %collective-permute-start.3) | collective-permute-done | bytes 375032 | tf_op jit(solution)/shard_map/ppermute | solution.py:17
  158.5 2.6 %collective-permute-start.5 = (f32[1,6,125,125]{2,3,1,0:T(8,128)S(1)}, f32[1,6,125,125]{2,3,1,0:T(8,128)S(1)}, u32[]{:S(2)}, u32[]{:S(2)}) collective-permute-start(f32[1,6,125,125]{2,3,1,0:T(8,128)S(1)} %collective-permute-done.3), channel_id=1, source_target_pairs={{0,4},{4,8},{8,12},{12,16},{16,20},{20,24},{24,28},{28,0},{1,5},{5... | collective-permute-start | bytes 1125008 | tf_op jit(solution)/shard_map/ppermute | solution.py:17
  161.7 1.9 collective-permute-done.2
  163.8 16.3 %collective-permute-done.5 = f32[1,6,125,125]{2,3,1,0:T(8,128)S(1)} collective-permute-done((f32[1,6,125,125]{2,3,1,0:T(8,128)S(1)}, f32[1,6,125,125]{2,3,1,0:T(8,128)S(1)}, u32[]{:S(2)}, u32[]{:S(2)}) %collective-permute-start.5) | collective-permute-done | bytes 375032 | tf_op jit(solution)/shard_map/ppermute | solution.py:17
  180.1 2.5 %collective-permute-start.6 = (f32[1,6,125,125]{2,3,1,0:T(8,128)S(1)}, f32[1,6,125,125]{2,3,1,0:T(8,128)S(1)}, u32[]{:S(2)}, u32[]{:S(2)}) collective-permute-start(f32[1,6,125,125]{2,3,1,0:T(8,128)S(1)} %collective-permute-done.5), channel_id=1, source_target_pairs={{0,4},{4,8},{8,12},{12,16},{16,20},{20,24},{24,28},{28,0},{1,5},{5... | collective-permute-start | bytes 1125008 | tf_op jit(solution)/shard_map/ppermute | solution.py:17
  182.6 44.5 %all-reduce.3.cloned.1.call-done = f32[8,2,125,125]{3,1,2,0:T(2,128)} async-done(((f32[8,2,125,125]{3,1,2,0:T(2,128)}), f32[8,2,125,125]{3,1,2,0:T(2,128)}) %all-reduce.3.cloned.1.call-update) | async-done | bytes 1000016
  227.1 1.6 constant_dynamic-slice_fusion.10
  228.8 7.1 %all_gather.3 = f32[1,8,125,125]{3,0,2,1:T(1,128)S(1)} all-gather(f32[1,2,125,125]{3,0,2,1:T(1,128)S(1)} %copy.45), channel_id=1, replica_groups=mesh['row'=8,'col'=4] {'col'}, dimensions={1}, use_global_device_ids=true | all-gather | bytes 625000 | tf_op jit(solution)/shard_map/all_gather | solution.py:67
  238.7 1.0 copy.54
  (60 shorter events, 10.1 us)
Async XLA Ops:
  52.3 7.5 %copy-start = (f32[1,6,125,125]{3,0,2,1:T(1,128)S(1)}, f32[1,6,125,125]{3,0,2,1:T(1,128)}, u32[]{:S(2)}) copy-start(f32[1,6,125,125]{3,0,2,1:T(1,128)} %param.9) | copy-start | bytes 1125004
  52.3 7.8 %copy-start.1 = (s32[1,6]{1,0:T(1,128)S(1)}, s32[1,6]{1,0:T(1,128)}, u32[]{:S(2)}) copy-start(s32[1,6]{1,0:T(1,128)} %param.10) | copy-start | bytes 76
  52.3 54.7 %all-to-all-start = ((f32[8,2,2,125,125]{4,2,3,1,0:T(2,128)}), f32[8,2,2,125,125]{4,2,3,1,0:T(2,128)}, u32[]{:S(2)}, u32[]{:S(2)}) async-start(f32[8,2,2,125,125]{4,2,3,1,0:T(2,128)} %bitcast.140), calls=%async_computation | async-start | bytes 4096000 | tf_op jit(solution)/shard_map/all_to_all | solution.py:53
  59.8 167.3 %all-reduce.3.cloned.1.call-start = ((), (), s32[]{:S(2)}) async-start(), calls=%async_computation.1 | async-start | bytes 2048000
  60.3 62.4 %collective-permute-start.1 = (f32[1,6,125,125]{2,3,1,0:T(8,128)S(1)}, f32[1,6,125,125]{2,3,1,0:T(8,128)S(1)}, u32[]{:S(2)}, u32[]{:S(2)}) collective-permute-start(f32[1,6,125,125]{2,3,1,0:T(8,128)S(1)} %broadcast_multiply_fusion.1), channel_id=1, source_target_pairs={{0,4},{4,8},{8,12},{12,16},{16,20},{20,24},{24,28},{28,0},{1,5},{5... | collective-permute-start | bytes 1125008 | tf_op jit(solution)/shard_map/ppermute | solution.py:17
  118.8 42.3 %copy-start.2 = (u32[32]{0:T(128)S(1)}, u32[32]{0:T(128)}, u32[]{:S(2)}) copy-start(u32[32]{0:T(128)} %constant.162) | copy-start | bytes 388
  120.2 28.0 %collective-permute-start = (f32[1,6,125,125]{2,3,1,0:T(8,128)S(1)}, f32[1,6,125,125]{2,3,1,0:T(8,128)S(1)}, u32[]{:S(2)}, u32[]{:S(2)}) collective-permute-start(f32[1,6,125,125]{2,3,1,0:T(8,128)S(1)} %broadcast_multiply_fusion.1), channel_id=1, source_target_pairs={{0,28},{4,0},{8,4},{12,8},{16,12},{20,16},{24,20},{28,24},{1,29},{... | collective-permute-start | bytes 1125008 | tf_op jit(solution)/shard_map/ppermute | solution.py:19
  122.7 35.7 %collective-permute-start.3 = (f32[1,6,125,125]{2,3,1,0:T(8,128)S(1)}, f32[1,6,125,125]{2,3,1,0:T(8,128)S(1)}, u32[]{:S(2)}, u32[]{:S(2)}) collective-permute-start(f32[1,6,125,125]{2,3,1,0:T(8,128)S(1)} %collective-permute-done.1), channel_id=1, source_target_pairs={{0,4},{4,8},{8,12},{12,16},{16,20},{20,24},{24,28},{28,0},{1,5},{5... | collective-permute-start | bytes 1125008 | tf_op jit(solution)/shard_map/ppermute | solution.py:17
  148.2 15.4 %collective-permute-start.2 = (f32[1,6,125,125]{2,3,1,0:T(8,128)S(1)}, f32[1,6,125,125]{2,3,1,0:T(8,128)S(1)}, u32[]{:S(2)}, u32[]{:S(2)}) collective-permute-start(f32[1,6,125,125]{2,3,1,0:T(8,128)S(1)} %collective-permute-done), channel_id=1, source_target_pairs={{0,28},{4,0},{8,4},{12,8},{16,12},{20,16},{24,20},{28,24},{1,29},{... | collective-permute-start | bytes 1125008 | tf_op jit(solution)/shard_map/ppermute | solution.py:19
  158.5 21.6 %collective-permute-start.5 = (f32[1,6,125,125]{2,3,1,0:T(8,128)S(1)}, f32[1,6,125,125]{2,3,1,0:T(8,128)S(1)}, u32[]{:S(2)}, u32[]{:S(2)}) collective-permute-start(f32[1,6,125,125]{2,3,1,0:T(8,128)S(1)} %collective-permute-done.3), channel_id=1, source_target_pairs={{0,4},{4,8},{8,12},{12,16},{16,20},{20,24},{24,28},{28,0},{1,5},{5... | collective-permute-start | bytes 1125008 | tf_op jit(solution)/shard_map/ppermute | solution.py:17
  163.5 74.4 %collective-permute-start.4 = (f32[1,6,125,125]{2,3,1,0:T(8,128)S(1)}, f32[1,6,125,125]{2,3,1,0:T(8,128)S(1)}, u32[]{:S(2)}, u32[]{:S(2)}) collective-permute-start(f32[1,6,125,125]{2,3,1,0:T(8,128)S(1)} %collective-permute-done.2), channel_id=1, source_target_pairs={{0,28},{4,0},{8,4},{12,8},{16,12},{20,16},{24,20},{28,24},{1,29},{... | collective-permute-start | bytes 1125008 | tf_op jit(solution)/shard_map/ppermute | solution.py:19
  180.1 58.2 %collective-permute-start.6 = (f32[1,6,125,125]{2,3,1,0:T(8,128)S(1)}, f32[1,6,125,125]{2,3,1,0:T(8,128)S(1)}, u32[]{:S(2)}, u32[]{:S(2)}) collective-permute-start(f32[1,6,125,125]{2,3,1,0:T(8,128)S(1)} %collective-permute-done.5), channel_id=1, source_target_pairs={{0,4},{4,8},{8,12},{12,16},{16,20},{20,24},{24,28},{28,0},{1,5},{5... | collective-permute-start | bytes 1125008 | tf_op jit(solution)/shard_map/ppermute | solution.py:17
Sparse Core Ops, SparseCore 0:
  120.3 106.7 all-reduce.2
